TPU v7x, 256 devices: a whole 4x4x8 slice. The times are simulated.
256 devices in a mesh: mp: 16 (over z, core), hidden: 16 (over y, x).
Axes of the slice: x: 4, y: 4, z: 8, core: 2. Of those that a mesh axis runs over, the one named last changes fastest.
Arguments:
- tokens: bfloat16 [512, 8192], P('hidden', 'mp'), may hold values from -6 to 6
- grad_output: bfloat16 [512, 8192], P('hidden', 'mp'), may hold values from -6 to 6
- gate_weight: bfloat16 [8192, 28672], P('mp', 'hidden'), may hold values from -0.0625 to 0.0625
- up_weight: bfloat16 [8192, 28672], P('mp', 'hidden'), may hold values from -0.0625 to 0.0625
- down_weight: bfloat16 [28672, 8192], P('hidden', 'mp'), may hold values from -0.03125 to 0.03125
Outputs:
- grad_input: bfloat16 [512, 8192], P('hidden', 'mp')
- sal_gate: bfloat16 [8192, 28672], P('mp', 'hidden')
- sal_up: bfloat16 [8192, 28672], P('mp', 'hidden')
- sal_down: bfloat16 [28672, 8192], P('hidden', 'mp')
All inputs are finite; a program needn't handle non-finite values.
Results may differ from a plain program's by a relative error of at most 0.0049.
Values may be sent and summed in bfloat16 or wider, within the bound.
A program may use at most 128 MiB of HBM per device.

v0:
```python
import jax
import jax.numpy as jnp
from jax import lax
from jax.sharding import PartitionSpec as P


def activate(gate, up, grad_hidden):
    sig = jax.nn.sigmoid(gate)
    silu_gate = gate * sig
    hidden = (silu_gate * up).astype(jnp.bfloat16)
    grad_gate = (grad_hidden * up * sig * (1.0 + gate * (1.0 - sig))).astype(jnp.bfloat16)
    grad_up = (grad_hidden * silu_gate).astype(jnp.bfloat16)
    return (hidden, grad_gate, grad_up)


def saliency(weight, left, right):
    grads = lax.dot_general(
        left, right, (((0,), (0,)), ((), ())), preferred_element_type=jnp.float32
    )
    return jnp.abs(weight.astype(jnp.float32) * grads).astype(jnp.bfloat16)


def local(tokens, grad_output, gate_weight, up_weight, down_weight):
    tok_all, grad_all = (
        lax.all_gather(tokens, "hidden", axis=0, tiled=True),
        lax.all_gather(grad_output, "hidden", axis=0, tiled=True),
    )
    gate_part = jnp.dot(tok_all, gate_weight, preferred_element_type=jnp.float32)
    up_part = jnp.dot(tok_all, up_weight, preferred_element_type=jnp.float32)
    hid_part = lax.dot_general(
        grad_all, down_weight, (((1,), (1,)), ((), ())), preferred_element_type=jnp.float32
    )
    gate, up, grad_hidden = lax.psum((gate_part, up_part, hid_part), "mp")
    hidden, grad_gate, grad_up = activate(gate, up, grad_hidden)
    sal_down = saliency(down_weight, hidden, grad_all)
    sal_gate = saliency(gate_weight, tok_all, grad_gate)
    sal_up = saliency(up_weight, tok_all, grad_up)
    first = lax.dot_general(
        grad_gate, gate_weight, (((1,), (1,)), ((), ())), preferred_element_type=jnp.float32
    )
    second = lax.dot_general(
        grad_up, up_weight, (((1,), (1,)), ((), ())), preferred_element_type=jnp.float32
    )
    grad_input = lax.psum_scatter(first + second, "hidden", scatter_dimension=0, tiled=True).astype(
        jnp.bfloat16
    )
    return (grad_input, sal_gate, sal_up, sal_down)


def solution(mesh):
    return jax.shard_map(
        local,
        mesh=mesh,
        in_specs=(
            P("hidden", "mp"),
            P("hidden", "mp"),
            P("mp", "hidden"),
            P("mp", "hidden"),
            P("hidden", "mp"),
        ),
        out_specs=(P("hidden", "mp"), P("mp", "hidden"), P("mp", "hidden"), P("hidden", "mp")),
        check_vma=False,
    )
```

profile of v0, /device:TPU:1, one launch (start us, length us, event | category | flops | bytes accessed | tf_op | source)
XLA Modules:
  0.0 307.6 jit_solution(12096366786125458018)
XLA Ops:
  7.2 0.0 all-reduce.3.cloned.1.call-start
  7.2 20.0 %all_gather.7 = bf16[512,512]{1,0:T(8,128)(2,1)S(1)} all-gather(bf16[32,512]{1,0:T(8,128)(2,1)} %param.5), channel_id=1, replica_groups=mesh['mp'=16,'hidden'=16] {'hidden'}, dimensions={0}, use_global_device_ids=true | all-gather | bytes 557056 | tf_op jit(solution)/shard_map/all_gather | solution.py:25
  27.2 0.0 copy-start
  27.2 4.6 %fusion.8 = f32[512,1792]{1,0:T(8,128)} fusion(bf16[512,512]{1,0:T(8,128)(2,1)S(1)} %all_gather.7, bf16[512,1792]{1,0:T(8,128)(2,1)} %param.8), kind=kOutput, calls=%fused_computation.15 | convolution fusion | flops 939524096 | bytes 6029312 | tf_op jit(solution)/shard_map/dot_general | solution.py:29
  31.8 0.0 copy-done
  31.8 0.0 copy-start.8
  31.8 0.0 copy-start.6
  31.8 3.0 fusion.9
  34.8 0.0 copy-done.8
  34.8 17.4 %all_gather.6 = bf16[512,512]{1,0:T(8,128)(2,1)S(1)} all-gather(bf16[32,512]{1,0:T(8,128)(2,1)S(1)} %copy-done.8), channel_id=1, replica_groups=mesh['mp'=16,'hidden'=16] {'hidden'}, dimensions={0}, use_global_device_ids=true | all-gather | bytes 557056 | tf_op jit(solution)/shard_map/all_gather | solution.py:26
  52.2 0.0 copy-done.6
  52.2 3.0 fusion.7
  55.2 0.0 all-reduce.3.cloned.1.call-update
  55.2 0.0 reduce-scatter.2.cloned.1.call-start
  55.3 157.6 %all-reduce.3.cloned.1.call-done = (f32[512,1792]{1,0:T(8,128)}, f32[512,1792]{1,0:T(8,128)}, f32[512,1792]{1,0:T(8,128)}) async-done(((f32[512,1792]{1,0:T(8,128)}, f32[512,1792]{1,0:T(8,128)}, f32[512,1792]{1,0:T(8,128)}), (f32[512,1792]{1,0:T(8,128)}, f32[512,1792]{1,0:T(8,128)}, f32[512,1792]{1,0:T(8,128)})) %all-reduce.3.cloned.1.call-update) | async-done | bytes 11010064 | tf_op jit(solution)/shard_map/psum | solution.py:33
  212.9 5.1 %multiply_convert_fusion.1 = (bf16[512,1792]{1,0:T(8,128)(2,1)S(1)}, bf16[512,1792]{1,0:T(8,128)(2,1)S(1)}) fusion(f32[512,1792]{1,0:T(8,128)} %get-tuple-element.9, f32[512,1792]{1,0:T(8,128)} %get-tuple-element.8, f32[512,1792]{1,0:T(8,128)} %get-tuple-element.10), kind=kLoop, calls=%fused_computation.8 | loop fusion | flops 11927552 | bytes 14680064 | tf_op jit(solution)/shard_map/convert_element_type | solution.py:12
  218.0 0.0 copy-start.4
  218.0 0.0 copy-start.2
  218.0 0.0 copy-start.1
  218.0 1.1 fusion.10
  219.2 0.1 copy-done.4
  219.2 0.7 copy-done.2
  219.9 1.0 copy-done.1
  220.8 2.1 convolution_add_fusion
  222.9 0.0 reduce-scatter.2.cloned.1.call-update
  223.0 2.3 copy.9
  225.3 0.0 copy-start.5
  225.3 4.0 %copy.10 = bf16[512,1792]{0,1:T(8,128)(2,1)} copy(bf16[512,1792]{1,0:T(8,128)(2,1)} %param.8) | data formatting | bytes 3670016 | tf_op args[3]
  229.3 0.0 copy-done.5
  229.3 3.9 %fusion.3 = bf16[512,1792]{0,1:T(8,128)(2,1)} fusion(bf16[512,1792]{0,1:T(8,128)(2,1)} %copy.9, bf16[512,1792]{1,0:T(8,128)(2,1)S(1)} %copy-done.5, bf16[512,512]{1,0:T(8,128)(2,1)S(1)} %all_gather.7), kind=kOutput, calls=%fused_computation.5 | convolution fusion | flops 943194112 | bytes 6029312 | tf_op jit(solution)/shard_map/dot_general | solution.py:17
  233.2 0.0 copy-start.3
  233.2 3.9 %copy.11 = bf16[512,1792]{1,0:T(8,128)(2,1)} copy(bf16[512,1792]{0,1:T(8,128)(2,1)} %fusion.3) | data formatting | bytes 3670016
  237.1 0.0 copy-done.3
  237.1 3.9 %fusion.1 = bf16[512,1792]{0,1:T(8,128)(2,1)} fusion(bf16[512,1792]{0,1:T(8,128)(2,1)} %copy.10, bf16[512,1792]{1,0:T(8,128)(2,1)S(1)} %copy-done.3, bf16[512,512]{1,0:T(8,128)(2,1)S(1)} %all_gather.7), kind=kOutput, calls=%fused_computation.2 | convolution fusion | flops 943194112 | bytes 6029312 | tf_op jit(solution)/shard_map/dot_general | solution.py:17
  241.0 0.0 copy-start.7
  241.0 3.9 %copy.12 = bf16[512,1792]{1,0:T(8,128)(2,1)} copy(bf16[512,1792]{0,1:T(8,128)(2,1)} %fusion.1) | data formatting | bytes 3670016
  244.9 0.0 copy-done.7
  244.9 6.1 %abs_convert_fusion = bf16[1792,512]{1,0:T(8,128)(2,1)} fusion(bf16[1792,512]{1,0:T(8,128)(2,1)S(1)} %copy-done.7, bf16[512,512]{1,0:T(8,128)(2,1)S(1)} %all_gather.6, f32[512,1792]{1,0:T(8,128)} %get-tuple-element.10, f32[512,1792]{1,0:T(8,128)} %get-tuple-element.8), kind=kOutput, calls=%fused_computation.6 | convolution fusion | flops 948699136 | bytes 11534336 | tf_op jit(solution)/shard_map/dot_general | solution.py:17
  251.0 48.3 %reduce-scatter.2.cloned.1.call-done = f32[32,512]{1,0:T(8,128)} async-done(((f32[512,512]{1,0:T(8,128)}), f32[32,512]{1,0:T(8,128)}) %reduce-scatter.2.cloned.1.call-update) | async-done | bytes 65552 | tf_op jit(solution)/shard_map/reduce_scatter | solution.py:44
  299.3 1.5 convert_element_type.32
Async XLA Ops:
  7.2 205.7 %all-reduce.3.cloned.1.call-start = ((), (), s32[]{:S(2)}) async-start(), calls=%async_computation.2 | async-start | bytes 22020096 | tf_op jit(solution)/shard_map/psum | solution.py:33
  27.2 4.6 %copy-start = (bf16[512,1792]{1,0:T(8,128)(2,1)S(1)}, bf16[512,1792]{1,0:T(8,128)(2,1)}, u32[]{:S(2)}) copy-start(bf16[512,1792]{1,0:T(8,128)(2,1)} %param.7) | copy-start | bytes 5505028
  31.8 3.0 copy-start.8
  31.8 20.4 %copy-start.6 = (bf16[1792,512]{1,0:T(8,128)(2,1)S(1)}, bf16[1792,512]{1,0:T(8,128)(2,1)}, u32[]{:S(2)}) copy-start(bf16[1792,512]{1,0:T(8,128)(2,1)} %param.9) | copy-start | bytes 5505028
  55.2 244.1 %reduce-scatter.2.cloned.1.call-start = ((), (), s32[]{:S(2)}) async-start(), calls=%async_computation.1 | async-start | bytes 1114112 | tf_op jit(solution)/shard_map/reduce_scatter | solution.py:44
  218.0 1.2 copy-start.4
  218.0 1.9 copy-start.2
  218.0 2.8 copy-start.1
  225.3 4.0 %copy-start.5 = (bf16[512,1792]{1,0:T(8,128)(2,1)S(1)}, bf16[512,1792]{1,0:T(8,128)(2,1)}, u32[]{:S(2)}) copy-start(bf16[512,1792]{1,0:T(8,128)(2,1)} %copy-done.4) | copy-start | bytes 5505028
  233.2 3.9 %copy-start.3 = (bf16[512,1792]{1,0:T(8,128)(2,1)S(1)}, bf16[512,1792]{1,0:T(8,128)(2,1)}, u32[]{:S(2)}) copy-start(bf16[512,1792]{1,0:T(8,128)(2,1)} %copy-done.2) | copy-start | bytes 5505028
  241.0 3.9 %copy-start.7 = (bf16[1792,512]{1,0:T(8,128)(2,1)S(1)}, bf16[1792,512]{1,0:T(8,128)(2,1)}, u32[]{:S(2)}) copy-start(bf16[1792,512]{1,0:T(8,128)(2,1)} %param.9) | copy-start | bytes 5505028
Sparse Core Ops, SparseCore 0:
  55.3 157.4 all-reduce.2
  223.1 76.1 reduce-scatter.1
where the time goes:
time: 309 us; the launch traced here: 308 us
  waiting for transfers between devices  206 us (67%)
  blocking collectives  37.4 us (12%)
  matrix products  27.7 us (9%)
  local copies, waits for them, and re-layouts  15.9 us (5%)
  between operations  14.1 us (5%)
  other arithmetic  6.56 us (2%)
    psum x1, waiting for transfers between devices, local(): gate, up, grad_hidden = lax.psum((gate_part, up_part, hid_part), 'mp')  158 us
    reduce_scatter x1, waiting for transfers between devices, local(): lax.psum_scatter(first + second, 'hidden', scatter_dimension=0, tiled=True)  48.3 us
    all_gather x1, blocking collectives, local(): lax.all_gather(tokens, 'hidden', axis=0, tiled=True)  20 us
    all_gather x1, blocking collectives, local(): lax.all_gather(grad_output, 'hidden', axis=0, tiled=True)  17.4 us
    unnamed x22, local copies, waits for them, and re-layouts  15.9 us
    dot_general x3, matrix products, saliency(): lax.dot_general(left, right, (((0,), (0,)), ((), ())), preferred_element_...  13.9 us
  transfers between devices with their start and end apart: 2, of which 2 were waited for; matrix products, arithmetic and copies ran while one was open for 9% of the time, Pallas kernels for 0%

commit v1 on v0

v1 whole, which is shorter than its diff:
```python
import jax
import jax.numpy as jnp
from jax import lax
from jax.experimental import pallas as pl
from jax.experimental.pallas import tpu as pltpu
from jax.sharding import PartitionSpec as P

MESH = pl.DeviceIdType.MESH
F32 = jnp.float32
BF16 = jnp.bfloat16
HALF = 896
PHASES = ((0, 512), (512, 384))
BLOCK = 64


def encode(value):
    return (value * jnp.abs(value)).astype(BF16)


def decode(sent):
    square = sent.astype(F32)
    size = jnp.abs(square)
    root = size * lax.rsqrt(jnp.maximum(size, 1e-36))
    return jnp.where(square < 0, -root, root)


def dot_nt(left, right):
    return lax.dot_general(left, right, (((1,), (1,)), ((), ())), preferred_element_type=F32)


def dot_tn(left, right):
    return lax.dot_general(left, right, (((0,), (0,)), ((), ())), preferred_element_type=F32)


def kernel(
    tok_ref, go_ref, wg_ref, wu_ref, wd_ref,
    gi_ref, sg_ref, su_ref, sd_ref,
    act_in, act_px, w_gu, w_d, px_gu, px_d,
    rs_send0, rs_send1, rs_recv0, rs_recv1, first0, first1,
    all0, all1, gi_send, gi_recv, out_gu, out_d,
    load_sem, px_send, px_recv, tok_send, tok_recv, share_send, share_recv,
    rs_ssem, rs_rsem, ag_ssem, ag_rsem, pair_send, pair_recv, gi_ssem, gi_rsem, out_sem,
):
    mp, hid = lax.axis_index("mp"), lax.axis_index("hidden")
    z, core = mp // 2, mp % 2
    y, x = hid // 4, hid % 4
    rs_send, rs_recv, first, gathered = (rs_send0, rs_send1), (rs_recv0, rs_recv1), (first0, first1), (all0, all1)

    def remote(src, dst, ssem, rsem, device):
        return pltpu.make_async_remote_copy(
            src_ref=src, dst_ref=dst, send_sem=ssem, recv_sem=rsem, device_id=device, device_id_type=MESH
        )

    def ring(way):
        return (lax.rem(z + 1 + 6 * way, 8) * 2 + core, hid)

    partner = (z * 2 + (1 - core), hid)

    def in_plane(j):
        return (mp, lax.rem(hid + j, 16))

    def along(a, axis, step):
        if (a + axis) % 2 == 0:
            return (mp, y * 4 + lax.rem(x + step, 4))
        return (mp, lax.rem(y + step, 4) * 4 + x)

    own_col = pl.multiple_of(core * HALF, 128)
    other_col = pl.multiple_of((1 - core) * HALF, 128)

    loads = []

    def load(src, dst):
        copy = pltpu.make_async_copy(src, dst, load_sem.at[len(loads)])
        copy.start()
        loads.append(copy)

    load(tok_ref, act_in.at[0, y, x])
    load(go_ref, act_in.at[1, y, x])
    for half, col in ((0, own_col), (1, other_col)):
        load(wg_ref.at[:, pl.ds(col, HALF)], w_gu.at[half, 0])
        load(wu_ref.at[:, pl.ds(col, HALF)], w_gu.at[half, 1])
        load(wd_ref.at[pl.ds(col, HALF), :], w_d.at[half])

    barrier = pltpu.get_barrier_semaphore()
    for j in range(1, 16):
        pl.semaphore_signal(barrier, inc=1, device_id=in_plane(j), device_id_type=MESH)
    for device in (ring(0), ring(1), partner):
        pl.semaphore_signal(barrier, inc=1, device_id=device, device_id_type=MESH)
    pl.semaphore_wait(barrier, 18)

    sources = (tok_ref, go_ref)
    line_copies = []
    for a in range(2):
        for j, step in enumerate((1, 3, 2)):
            copy = remote(
                sources[a], act_in.at[a, y, x], tok_send.at[a, j], tok_recv.at[a, j], along(a, 0, step)
            )
            copy.start()
            line_copies.append(copy)
    px_copies = []
    for i, (src, dst) in enumerate((
        (wg_ref.at[:, pl.ds(other_col, HALF)], px_gu.at[0]),
        (wu_ref.at[:, pl.ds(other_col, HALF)], px_gu.at[1]),
        (wd_ref.at[pl.ds(other_col, HALF), :], px_d),
    )):
        copy = remote(src, dst, px_send.at[i], px_recv.at[i], partner)
        copy.start()
        px_copies.append(copy)

    def line(a, step, part=None):
        if a == 0:
            at = lax.rem(y + step, 4)
            return act_in.at[0, at] if part is None else act_in.at[0, at, 2 * part : 2 * part + 2]
        at = lax.rem(x + step, 4)
        return act_in.at[1, :, at] if part is None else act_in.at[1, 2 * part : 2 * part + 2, at]

    def line_px(a, step):
        if a == 0:
            return act_px.at[0, lax.rem(y + step, 4)]
        return act_px.at[1, :, lax.rem(x + step, 4)]

    def share(a, step):
        copy = remote(
            line(a, step), line_px(a, step), share_send.at[a, step], share_recv.at[a, step], partner
        )
        copy.start()
        share_copies.append(copy)

    share_copies = []
    wide = {}
    for a in range(2):
        loads[a].wait()
        for j in range(3):
            line_copies[3 * a + j].wait_recv()
        for way, part in ((0, 0), (1, 1), (0, 1), (1, 0)):
            i = 3 + 2 * way + part
            copy = remote(
                line(a, 0, part), line(a, 0, part), tok_send.at[a, i], tok_recv.at[a, i],
                along(a, 1, 1 if way == 0 else 3),
            )
            copy.start()
            wide[a, way, part] = copy
        share(a, 0)
    far = {}
    for a in range(2):
        for way in range(2):
            wide[a, way, way].wait_recv()
            step = 3 if way == 0 else 1
            i = 7 + way
            copy = remote(
                line(a, step, way), line(a, step, way), tok_send.at[a, i], tok_recv.at[a, i],
                along(a, 1, 1 if way == 0 else 3),
            )
            copy.start()
            far[a, way] = copy
    for a in range(2):
        for way in range(2):
            wide[a, way, 1 - way].wait_recv()
            share(a, 3 if way == 0 else 1)
    for copy in loads[2:]:
        copy.wait()
    for p in range(2):
        width = PHASES[p][1]
        for m in range(3):
            rs_recv[p][0, 0, m, 32:64, :] = jnp.zeros((32, width), BF16)
            rs_recv[p][1, 0, m, 0:32, :] = jnp.zeros((32, width), BF16)
    for copy in px_copies:
        copy.wait_recv()
    for a in range(2):
        far[a, 0].wait_recv()
        far[a, 1].wait_recv()
        share(a, 2)
    for copy in share_copies:
        copy.wait_recv()

    def partial(p, m, d):
        c0, width = PHASES[p]
        a = 1 if m == 2 else 0
        rows = (d // 2, pl.ds(lax.rem(d, 2) * 2, 2))
        mine = act_in[a, rows[0], rows[1]].reshape(BLOCK, 512)
        theirs = act_px[a, rows[0], rows[1]].reshape(BLOCK, 512)
        if m == 2:
            return dot_nt(mine, w_d[0, c0 : c0 + width, :]) + dot_nt(theirs, px_d[c0 : c0 + width, :])
        return jnp.dot(mine, w_gu[0, m, :, c0 : c0 + width], preferred_element_type=F32) + jnp.dot(
            theirs, px_gu[m, :, c0 : c0 + width], preferred_element_type=F32
        )

    def first_copy(p, way, m):
        rows = slice(32 * way, 32 * way + 32)
        return remote(
            first[p].at[m, rows], rs_recv[p].at[way, 0, m, rows],
            rs_ssem.at[p, way, 0, m], rs_rsem.at[p, way, 0, m], ring(way),
        )

    def next_copy(p, way, step, m):
        return remote(
            rs_send[p].at[way, step - 1, m], rs_recv[p].at[way, step, m],
            rs_ssem.at[p, way, step, m], rs_rsem.at[p, way, step, m], ring(way),
        )

    def reduce_first(p):
        for m in range(3):
            first[p][m] = encode(partial(p, m, lax.rem(z + 4, 8)))
            for way in range(2):
                first_copy(p, way, m).start()

    def reduce_rest(p):
        def body(t, _):
            way, step = lax.rem(t, 2), t // 2 + 1
            distance = 4 - step
            d = lax.rem(z + distance + way * (8 - 2 * distance), 8)
            for m in range(3):
                mine = partial(p, m, d)

                @pl.when(step == 1)
                def _():
                    @pl.when(way == 0)
                    def _():
                        first_copy(p, 0, m).wait_recv()

                    @pl.when(way == 1)
                    def _():
                        first_copy(p, 1, m).wait_recv()

                @pl.when(step > 1)
                def _():
                    next_copy(p, way, step - 1, m).wait_recv()

                rs_send[p][way, step - 1, m] = encode(mine + decode(rs_recv[p][way, step - 1, m]))
                next_copy(p, way, step, m).start()
            return 0

        lax.fori_loop(0, 6, body, 0)

    own_rows = pl.ds(pl.multiple_of(z * BLOCK, BLOCK), BLOCK)

    def activate(p):
        sums = []
        for m in range(3):
            mine = partial(p, m, z)
            for way in range(2):
                next_copy(p, way, 3, m).wait_recv()
            sums.append(mine + decode(rs_recv[p][0, 3, m]) + decode(rs_recv[p][1, 3, m]))
        gate, up, grad_hidden = sums
        sig = jax.nn.sigmoid(gate)
        silu_gate = gate * sig
        gathered[p][0, 0, own_rows] = (silu_gate * up).astype(BF16)
        gathered[p][0, 1, own_rows] = (grad_hidden * up * sig * (1.0 + gate * (1.0 - sig))).astype(BF16)
        gathered[p][0, 2, own_rows] = (grad_hidden * silu_gate).astype(BF16)

    def block_of(way, step):
        return lax.rem(z + (8 - step if way == 0 else step), 8)

    def spread_copy(p, way, step, m):
        start = block_of(way, step) * BLOCK
        count = BLOCK
        if step == 3:
            start, count = start + 32 * way, 32
        rows = pl.ds(pl.multiple_of(start, 32), count)
        ref = gathered[p].at[0, m, rows]
        return remote(ref, ref, ag_ssem.at[p, way, step, m], ag_rsem.at[p, way, step, m], ring(way))

    def pair_copy(p, k):
        d = lax.rem(z + (0, 7, 6, 5, 1, 2, 3, 4)[k], 8)
        rows = pl.ds(pl.multiple_of(d * BLOCK, BLOCK), BLOCK)
        return remote(
            gathered[p].at[0, :, rows], gathered[p].at[1, :, rows], pair_send.at[p, k], pair_recv.at[p, k], partner
        )

    def spread_first(p):
        for m in range(3):
            for way in range(2):
                spread_copy(p, way, 0, m).start()
        pair_copy(p, 0).start()

    def spread_next(p, step):
        for m in range(3):
            for way in range(2):
                spread_copy(p, way, step - 1, m).wait_recv()
                spread_copy(p, way, step, m).start()
        pair_copy(p, step).start()
        pair_copy(p, 3 + step).start()

    def spread_last(p):
        for m in range(3):
            for way in range(2):
                spread_copy(p, way, 3, m).wait_recv()
        pair_copy(p, 7).start()

    def grad_in(half, mat, p):
        c0, width = PHASES[p]
        cols = slice(c0, c0 + width)
        right = gathered[p][half, 1 + mat]
        tokens = act_in[0].reshape(512, 512)
        grads = dot_tn(tokens, right)
        out_gu[half, mat, :, cols] = jnp.abs(w_gu[half, mat, :, cols].astype(F32) * grads).astype(BF16)

    def saliency_gu(p, mat):
        def body(half, _):
            grad_in(half, mat, p)
            return 0

        lax.fori_loop(0, 2, body, 0)

    def saliency_d(p):
        c0, width = PHASES[p]

        def body(half, _):
            grads = dot_tn(gathered[p][half, 0], act_in[1].reshape(512, 512))
            rows = slice(c0, c0 + width)
            out_d[half, rows, :] = jnp.abs(w_d[half, rows, :].astype(F32) * grads).astype(BF16)
            return 0

        lax.fori_loop(0, 2, body, 0)

    outs = []

    def store(p, m):
        c0, width = PHASES[p]
        for half, base in ((0, own_col), (1, other_col)):
            at = pl.ds(pl.multiple_of(base + c0, 128), width)
            if m == 2:
                src, dst = out_d.at[half, c0 : c0 + width, :], sd_ref.at[at, :]
            else:
                src, dst = out_gu.at[half, m, :, c0 : c0 + width], (sg_ref, su_ref)[m].at[:, at]
            copy = pltpu.make_async_copy(src, dst, out_sem.at[p, m, half])
            copy.start()
            outs.append(copy)

    def gi_copy(d, part):
        dest = 2 * d + part
        return remote(
            gi_send.at[d, 32 * part : 32 * part + 32], gi_recv.at[hid],
            gi_ssem.at[d, part], gi_rsem.at[hid], (mp, dest),
        )

    def input_grad(d):
        rows = pl.ds(pl.multiple_of(d * BLOCK, BLOCK), BLOCK)
        total = jnp.zeros((BLOCK, 512), F32)
        for p in range(2):
            c0, width = PHASES[p]
            for half in range(2):
                for mat in range(2):
                    total += dot_nt(gathered[p][half, 1 + mat, rows], w_gu[half, mat, :, c0 : c0 + width])
        gi_send[d] = encode(total)
        for part in range(2):
            @pl.when(hid != 2 * d + part)
            def _():
                gi_copy(d, part).start()

    reduce_first(0)
    reduce_rest(0)
    reduce_first(1)
    activate(0)
    reduce_rest(1)
    spread_first(0)
    activate(1)
    for step in (1, 2, 3):
        spread_next(0, step)
    spread_first(1)
    spread_last(0)
    spread_next(1, 1)
    for k in range(8):
        pair_copy(0, k).wait_recv()
    saliency_gu(0, 0)
    store(0, 0)
    spread_next(1, 2)
    saliency_gu(0, 1)
    store(0, 1)
    spread_next(1, 3)
    saliency_d(0)
    store(0, 2)

    for k in range(7):
        pair_copy(1, k).wait_recv()

    def near(j, _):
        input_grad(lax.rem(z + 5 + j, 8))
        return 0

    lax.fori_loop(0, 7, near, 0)
    spread_last(1)
    pair_copy(1, 7).wait_recv()
    input_grad(lax.rem(z + 4, 8))
    for m in range(2):
        saliency_gu(1, m)
        store(1, m)
    saliency_d(1)
    store(1, 2)

    total = decode(gi_send[hid // 2, pl.ds(pl.multiple_of(lax.rem(hid, 2) * 32, 32), 32)])
    for j in range(1, 16):
        slot = lax.rem(hid + j, 16)
        remote(
            gi_send.at[0, 0:32], gi_recv.at[slot], gi_ssem.at[0, 0], gi_rsem.at[slot], in_plane(j)
        ).wait_recv()
        total += decode(gi_recv[slot])
    gi_ref[...] = total.astype(BF16)

    for copy in line_copies + px_copies + share_copies + list(wide.values()) + list(far.values()):
        copy.wait_send()
    for p in range(2):
        for way in range(2):
            for m in range(3):
                first_copy(p, way, m).wait_send()
                for step in (1, 2, 3):
                    next_copy(p, way, step, m).wait_send()
                for step in range(4):
                    spread_copy(p, way, step, m).wait_send()
        for k in range(8):
            pair_copy(p, k).wait_send()

    def sent(d, _):
        for part in range(2):
            @pl.when(hid != 2 * d + part)
            def _():
                gi_copy(d, part).wait_send()
        return 0

    lax.fori_loop(0, 8, sent, 0)
    for copy in outs:
        copy.wait()


def local(tokens, grad_output, gate_weight, up_weight, down_weight):
    anywhere = pl.BlockSpec(memory_space=pl.ANY)
    dma = pltpu.SemaphoreType.DMA
    sizes = [width for _, width in PHASES]
    return pl.pallas_call(
        kernel,
        out_shape=(
            jax.ShapeDtypeStruct((32, 512), BF16),
            jax.ShapeDtypeStruct((512, 1792), BF16),
            jax.ShapeDtypeStruct((512, 1792), BF16),
            jax.ShapeDtypeStruct((1792, 512), BF16),
        ),
        in_specs=[anywhere] * 5,
        out_specs=(pl.BlockSpec(memory_space=pltpu.VMEM), anywhere, anywhere, anywhere),
        scratch_shapes=[
            pltpu.VMEM((2, 4, 4, 32, 512), BF16),
            pltpu.VMEM((2, 4, 4, 32, 512), BF16),
            pltpu.VMEM((2, 2, 512, HALF), BF16),
            pltpu.VMEM((2, HALF, 512), BF16),
            pltpu.VMEM((2, 512, HALF), BF16),
            pltpu.VMEM((HALF, 512), BF16),
            *[pltpu.VMEM((2, 3, 3, BLOCK, width), BF16) for width in sizes],
            *[pltpu.VMEM((2, 4, 3, BLOCK, width), BF16) for width in sizes],
            *[pltpu.VMEM((3, BLOCK, width), BF16) for width in sizes],
            *[pltpu.VMEM((2, 3, 512, width), BF16) for width in sizes],
            pltpu.VMEM((8, BLOCK, 512), BF16),
            pltpu.VMEM((16, 32, 512), BF16),
            pltpu.VMEM((2, 2, 512, HALF), BF16),
            pltpu.VMEM((2, HALF, 512), BF16),
            dma((8,)),
            dma((3,)),
            dma((3,)),
            dma((2, 9)),
            dma((2, 9)),
            dma((2, 4)),
            dma((2, 4)),
            dma((2, 2, 4, 3)),
            dma((2, 2, 4, 3)),
            dma((2, 2, 4, 3)),
            dma((2, 2, 4, 3)),
            dma((2, 8)),
            dma((2, 8)),
            dma((8, 2)),
            dma((16,)),
            dma((2, 3, 2)),
        ],
        compiler_params=pltpu.CompilerParams(
            collective_id=0, has_side_effects=True, vmem_limit_bytes=56 * 2**20
        ),
        cost_estimate=pl.CostEstimate(flops=7_516_192_768, bytes_accessed=11_010_048, transcendentals=2_000_000),
    )(tokens, grad_output, gate_weight, up_weight, down_weight)


def solution(mesh):
    return jax.shard_map(
        local,
        mesh=mesh,
        in_specs=(
            P("hidden", "mp"),
            P("hidden", "mp"),
            P("mp", "hidden"),
            P("mp", "hidden"),
            P("hidden", "mp"),
        ),
        out_specs=(P("hidden", "mp"), P("mp", "hidden"), P("mp", "hidden"), P("hidden", "mp")),
        check_vma=False,
    )
```

time: 309 us -> 117 us (0.38)
  waiting for transfers between devices: 206 us -> 0 us
  Pallas kernels: 0 us -> 107 us
  blocking collectives: 37.4 us -> 0 us
  matrix products: 27.7 us -> 0 us
  between operations: 14.1 us -> 0.64 us
  local copies, waits for them, and re-layouts: 15.9 us -> 7.75 us
  other arithmetic: 6.56 us -> 0 us
    psum x1 -> x0, waiting for transfers between devices: 158 us -> none  [local(): gate, up, grad_hidden = lax.psum((gate_part, up_part, hid_part), 'mp')]
    pallas_call x0 -> x1, Pallas kernels: none -> 107 us  [local(): pl.pallas_call(kernel, out_shape=(jax.ShapeDtypeStruct((32, 512), BF16),...]
    reduce_scatter x1 -> x0, waiting for transfers between devices: 48.3 us -> none  [local(): lax.psum_scatter(first + second, 'hidden', scatter_dimension=0, tiled=True)]
    all_gather x2 -> x0, blocking collectives: 37.4 us -> none  [the longest x1 20 us: local(): lax.all_gather(tokens, 'hidden', axis=0, tiled=True)]
    dot_general x8 -> x0, matrix products: 27.7 us -> none  [the longest x3 13.9 us: saliency(): lax.dot_general(left, right, (((0,), (0,)), ((), ())), preferred_element_...]
    unnamed x22 -> x8, local copies, waits for them, and re-layouts: 15.9 us -> 7.75 us
    convert_element_type x2 -> x0, other arithmetic: 6.56 us -> none  [the longest x1 5.1 us: activate(): grad_up = (grad_hidden * silu_gate).astype(jnp.bfloat16)]
  transfers between devices with their start and end apart: 2 -> 0, of which waited for: 2 -> 0; matrix products, arithmetic and copies ran while one was open for 9% -> 0% of each run, Pallas kernels for 0% -> 0%
where the time goes in v1:
time: 117 us; the launch traced here: 115 us
  Pallas kernels  107 us (91%)
  local copies, waits for them, and re-layouts  7.75 us (7%)
    pallas_call x1, Pallas kernels, local(): pl.pallas_call(kernel, out_shape=(jax.ShapeDtypeStruct((32, 512), BF16),...  107 us
    unnamed x8, local copies, waits for them, and re-layouts  7.75 us

profile of v1, /device:TPU:1, one launch (start us, length us, event | category | flops | bytes accessed | tf_op | source)
XLA Modules:
  0.0 115.1 jit_solution(4702520802261240128)
XLA Ops:
  0.6 106.7 %shard_map.84 = (bf16[32,512]{1,0:T(8,128)(2,1)}, bf16[512,1792]{1,0:T(8,128)(2,1)}, bf16[512,1792]{1,0:T(8,128)(2,1)}, bf16[1792,512]{1,0:T(8,128)(2,1)}) custom-call(bf16[32,512]{1,0:T(8,128)(2,1)} %tok_ref.1, bf16[32,512]{1,0:T(8,128)(2,1)} %go_ref.1, bf16[512,1792]{1,0:T(8,128)(2,1)} %wg_ref.1, bf16[512,1792]{1,0:T(8,128)(2,1)} %wu_ref.1, ...), custom_call_target="tpu_custom_call" | custom-call | flops 7516192768 | bytes 11010048 | tf_op jit(solution)/shard_map/pallas_call | solution.py:429
  107.4 1.4 %copy.13 = bf16[32,512]{1,0:T(8,128)(2,1)} copy(bf16[32,512]{1,0:T(8,128)(2,1)} %get-tuple-element.8) | data formatting | bytes 65536
  108.7 0.0 copy-start.1
  108.7 3.0 %copy.14 = bf16[512,1792]{1,0:T(8,128)(2,1)} copy(bf16[512,1792]{1,0:T(8,128)(2,1)} %get-tuple-element.9) | data formatting | bytes 3670016
  111.7 0.0 copy-done.1
  111.7 0.0 copy-start
  111.7 1.2 %copy.15 = bf16[512,1792]{1,0:T(8,128)(2,1)} copy(bf16[512,1792]{1,0:T(8,128)(2,1)S(1)} %copy-done.1) | data formatting | bytes 3670016
  112.9 0.9 copy-done
  113.9 1.2 %copy.16 = bf16[1792,512]{1,0:T(8,128)(2,1)} copy(bf16[1792,512]{1,0:T(8,128)(2,1)S(1)} %copy-done) | data formatting | bytes 3670016
Async XLA Ops:
  108.7 3.0 %copy-start.1 = (bf16[512,1792]{1,0:T(8,128)(2,1)S(1)}, bf16[512,1792]{1,0:T(8,128)(2,1)}, u32[]{:S(2)}) copy-start(bf16[512,1792]{1,0:T(8,128)(2,1)} %get-tuple-element.10) | copy-start | bytes 5505028
  111.7 2.2 %copy-start = (bf16[1792,512]{1,0:T(8,128)(2,1)S(1)}, bf16[1792,512]{1,0:T(8,128)(2,1)}, u32[]{:S(2)}) copy-start(bf16[1792,512]{1,0:T(8,128)(2,1)} %get-tuple-element.11) | copy-start | bytes 5505028

commit v2 on v1

v2 whole, which is shorter than its diff:
```python
import jax
import jax.numpy as jnp
from jax import lax
from jax.experimental import pallas as pl
from jax.experimental.pallas import tpu as pltpu
from jax.sharding import PartitionSpec as P

MESH = pl.DeviceIdType.MESH
F32 = jnp.float32
BF16 = jnp.bfloat16
HALF = 896
PHASES = ((0, 512), (512, 384))
BLOCK = 64


def encode(value):
    return (value * jnp.abs(value)).astype(BF16)


def decode(sent):
    square = sent.astype(F32)
    size = jnp.abs(square)
    root = size * lax.rsqrt(jnp.maximum(size, 1e-36))
    return jnp.where(square < 0, -root, root)


def dot_nt(left, right):
    return lax.dot_general(left, right, (((1,), (1,)), ((), ())), preferred_element_type=F32)


def dot_tn(left, right):
    return lax.dot_general(left, right, (((0,), (0,)), ((), ())), preferred_element_type=F32)


def kernel(
    tok_ref, go_ref, wg_ref, wu_ref, wd_ref,
    gi_ref, out_gu, out_d,
    act_in, act_px, w_gu, w_d, px_gu, px_d,
    rs_send0, rs_send1, rs_recv0, rs_recv1, first0, first1, mine0, mine1,
    all0, all1, gi_send, gi_recv,
    load_sem, px_send, px_recv, tok_send, tok_recv, share_send, share_recv,
    rs_ssem, rs_rsem, ag_ssem, ag_rsem, pair_send, pair_recv, gi_ssem, gi_rsem,
):
    mp, hid = lax.axis_index("mp"), lax.axis_index("hidden")
    z, core = mp // 2, mp % 2
    y, x = hid // 4, hid % 4
    rs_send, rs_recv, first = (rs_send0, rs_send1), (rs_recv0, rs_recv1), (first0, first1)
    own, gathered = (mine0, mine1), (all0, all1)

    def remote(src, dst, ssem, rsem, device):
        return pltpu.make_async_remote_copy(
            src_ref=src, dst_ref=dst, send_sem=ssem, recv_sem=rsem, device_id=device, device_id_type=MESH
        )

    def ring(way):
        return (lax.rem(z + 1 + 6 * way, 8) * 2 + core, hid)

    partner = (z * 2 + (1 - core), hid)

    def in_plane(j):
        return (mp, lax.rem(hid + j, 16))

    def along(f, axis, step):
        if (f + axis) % 2 == 0:
            return (mp, y * 4 + lax.rem(x + step, 4))
        return (mp, lax.rem(y + step, 4) * 4 + x)

    own_col = pl.multiple_of(core * HALF, 128)
    other_col = pl.multiple_of((1 - core) * HALF, 128)

    loads = []

    def load(src, dst):
        copy = pltpu.make_async_copy(src, dst, load_sem.at[len(loads)])
        copy.start()
        loads.append(copy)

    load(tok_ref, act_in.at[0, y, x])
    load(go_ref, act_in.at[1, y, x])
    for half, col in ((0, own_col), (1, other_col)):
        load(wg_ref.at[:, pl.ds(col, HALF)], w_gu.at[half, 0])
        load(wu_ref.at[:, pl.ds(col, HALF)], w_gu.at[half, 1])
        load(wd_ref.at[pl.ds(col, HALF), :], w_d.at[half])

    barrier = pltpu.get_barrier_semaphore()
    for j in range(1, 16):
        pl.semaphore_signal(barrier, inc=1, device_id=in_plane(j), device_id_type=MESH)
    for device in (ring(0), ring(1), partner):
        pl.semaphore_signal(barrier, inc=1, device_id=device, device_id_type=MESH)
    pl.semaphore_wait(barrier, 18)

    for p in range(2):
        width = PHASES[p][1]
        for m in range(3):
            rs_recv[p][0, 0, m, 32:64, :] = jnp.zeros((32, width), BF16)
            rs_recv[p][1, 0, m, 0:32, :] = jnp.zeros((32, width), BF16)

    sources = (tok_ref, go_ref)
    columns = (slice(0, 256), slice(256, 512))
    copies = []

    def begin(copy):
        copy.start()
        copies.append(copy)
        return copy

    near = {}
    for a in range(2):
        for f in range(2):
            for j, step in enumerate((1, 3, 2)):
                near[a, f, j] = begin(remote(
                    sources[a].at[:, columns[f]], act_in.at[a, y, x, :, columns[f]],
                    tok_send.at[a, f, j], tok_recv.at[a, f, j], along(f, 0, step),
                ))
    px_copies = []
    for i, (src, dst) in enumerate((
        (wg_ref.at[:, pl.ds(other_col, HALF)], px_gu.at[0]),
        (wu_ref.at[:, pl.ds(other_col, HALF)], px_gu.at[1]),
        (wd_ref.at[pl.ds(other_col, HALF), :], px_d),
    )):
        px_copies.append(begin(remote(src, dst, px_send.at[i], px_recv.at[i], partner)))

    def line(ref, a, f, step, part=None):
        span = slice(0, 4) if part is None else slice(2 * part, 2 * part + 2)
        if f == 0:
            return ref.at[a, lax.rem(y + step, 4), span, :, columns[0]]
        return ref.at[a, span, lax.rem(x + step, 4), :, columns[1]]

    shares = {}

    def share(a, f, step):
        shares[a, f, step] = begin(remote(
            line(act_in, a, f, step), line(act_px, a, f, step),
            share_send.at[a, f, step], share_recv.at[a, f, step], partner,
        ))

    wide, far = {}, {}

    def send_lines(a):
        loads[a].wait()
        for f in range(2):
            for j in range(3):
                near[a, f, j].wait_recv()
        for way, part in ((0, 0), (1, 1), (0, 1), (1, 0)):
            for f in range(2):
                i = 3 + 2 * way + part
                ref = line(act_in, a, f, 0, part)
                wide[a, f, way, part] = begin(remote(
                    ref, ref, tok_send.at[a, f, i], tok_recv.at[a, f, i], along(f, 1, 1 if way == 0 else 3)
                ))
        for f in range(2):
            share(a, f, 0)

    def pass_on(a):
        for way in range(2):
            for f in range(2):
                wide[a, f, way, way].wait_recv()
                ref = line(act_in, a, f, 3 if way == 0 else 1, way)
                far[a, f, way] = begin(remote(
                    ref, ref, tok_send.at[a, f, 7 + way], tok_recv.at[a, f, 7 + way],
                    along(f, 1, 1 if way == 0 else 3),
                ))
        for way in range(2):
            for f in range(2):
                wide[a, f, way, 1 - way].wait_recv()
                share(a, f, 3 if way == 0 else 1)

    def finish(a):
        for f in range(2):
            far[a, f, 0].wait_recv()
            far[a, f, 1].wait_recv()
            share(a, f, 2)
        for f in range(2):
            for step in range(4):
                shares[a, f, step].wait_recv()

    send_lines(0)
    pass_on(0)
    send_lines(1)
    for copy in loads[2:]:
        copy.wait()
    for copy in px_copies:
        copy.wait_recv()
    finish(0)

    def block(ref, a, d):
        return ref[a, d // 2, pl.ds(lax.rem(d, 2) * 2, 2)].reshape(BLOCK, 512)

    def partial(p, m, *ds):
        c0, width = PHASES[p]
        a = 1 if m == 2 else 0
        ours, theirs = [
            jnp.concatenate([block(ref, a, d) for d in ds]) if len(ds) > 1 else block(ref, a, ds[0])
            for ref in (act_in, act_px)
        ]
        if m == 2:
            return dot_nt(ours, w_d[0, c0 : c0 + width, :]) + dot_nt(theirs, px_d[c0 : c0 + width, :])
        return jnp.dot(ours, w_gu[0, m, :, c0 : c0 + width], preferred_element_type=F32) + jnp.dot(
            theirs, px_gu[m, :, c0 : c0 + width], preferred_element_type=F32
        )

    def first_copy(p, way, m):
        rows = slice(32 * way, 32 * way + 32)
        return remote(
            first[p].at[m, rows], rs_recv[p].at[way, 0, m, rows],
            rs_ssem.at[p, way, 0, m], rs_rsem.at[p, way, 0, m], ring(way),
        )

    def next_copy(p, way, step, m):
        return remote(
            rs_send[p].at[way, step - 1, m], rs_recv[p].at[way, step, m],
            rs_ssem.at[p, way, step, m], rs_rsem.at[p, way, step, m], ring(way),
        )

    pieces = ((0, 0), (0, 1), (1, 0), (1, 1), (0, 2), (1, 2))

    def reduce_first(p, m):
        first[p][m] = encode(partial(p, m, lax.rem(z + 4, 8)))
        for way in range(2):
            first_copy(p, way, m).start()

    def reduce_step(step, _):
        for p, m in pieces:
            both = partial(p, m, lax.rem(z + 4 - step, 8), lax.rem(z + 4 + step, 8))
            for way in range(2):
                @pl.when(step == 1)
                def _():
                    first_copy(p, way, m).wait_recv()

                @pl.when(step > 1)
                def _():
                    next_copy(p, way, step - 1, m).wait_recv()

                mine = both[BLOCK * way : BLOCK * way + BLOCK]
                rs_send[p][way, step - 1, m] = encode(mine + decode(rs_recv[p][way, step - 1, m]))
                next_copy(p, way, step, m).start()
        return 0

    own_rows = pl.ds(pl.multiple_of(z * BLOCK, BLOCK), BLOCK)

    def activate(p):
        sums = []
        for m in range(3):
            for way in range(2):
                next_copy(p, way, 3, m).wait_recv()
            sums.append(own[p][m] + decode(rs_recv[p][0, 3, m]) + decode(rs_recv[p][1, 3, m]))
        gate, up, grad_hidden = sums
        sig = jax.nn.sigmoid(gate)
        silu_gate = gate * sig
        gathered[p][0, 0, own_rows] = (silu_gate * up).astype(BF16)
        gathered[p][0, 1, own_rows] = (grad_hidden * up * sig * (1.0 + gate * (1.0 - sig))).astype(BF16)
        gathered[p][0, 2, own_rows] = (grad_hidden * silu_gate).astype(BF16)

    def block_of(way, step):
        return lax.rem(z + (8 - step if way == 0 else step), 8)

    def spread_copy(p, way, step, m):
        start = block_of(way, step) * BLOCK
        count = BLOCK
        if step == 3:
            start, count = start + 32 * way, 32
        rows = pl.ds(pl.multiple_of(start, 32), count)
        ref = gathered[p].at[0, m, rows]
        return remote(ref, ref, ag_ssem.at[p, way, step, m], ag_rsem.at[p, way, step, m], ring(way))

    def pair_copy(p, k):
        d = lax.rem(z + (0, 7, 6, 5, 1, 2, 3, 4)[k], 8)
        rows = pl.ds(pl.multiple_of(d * BLOCK, BLOCK), BLOCK)
        return remote(
            gathered[p].at[0, :, rows], gathered[p].at[1, :, rows], pair_send.at[p, k], pair_recv.at[p, k], partner
        )

    def spread_first(p):
        for m in range(3):
            for way in range(2):
                spread_copy(p, way, 0, m).start()
        pair_copy(p, 0).start()

    def spread_next(p, step):
        for m in range(3):
            for way in range(2):
                spread_copy(p, way, step - 1, m).wait_recv()
                spread_copy(p, way, step, m).start()
        pair_copy(p, step).start()
        pair_copy(p, 3 + step).start()

    def spread_last(p):
        for m in range(3):
            for way in range(2):
                spread_copy(p, way, 3, m).wait_recv()
        pair_copy(p, 7).start()

    def grad_in(half, mat, p):
        c0, width = PHASES[p]
        cols = slice(c0, c0 + width)
        right = gathered[p][half, 1 + mat]
        tokens = act_in[0].reshape(512, 512)
        grads = dot_tn(tokens, right)
        out_gu[half, mat, :, cols] = jnp.abs(w_gu[half, mat, :, cols].astype(F32) * grads).astype(BF16)

    def saliency_gu(p, mat):
        def body(half, _):
            grad_in(half, mat, p)
            return 0

        lax.fori_loop(0, 2, body, 0)

    def saliency_d(p):
        c0, width = PHASES[p]

        def body(half, _):
            grads = dot_tn(gathered[p][half, 0], act_in[1].reshape(512, 512))
            rows = slice(c0, c0 + width)
            out_d[half, rows, :] = jnp.abs(w_d[half, rows, :].astype(F32) * grads).astype(BF16)
            return 0

        lax.fori_loop(0, 2, body, 0)

    def gi_copy(d, part):
        dest = 2 * d + part
        return remote(
            gi_send.at[d, 32 * part : 32 * part + 32], gi_recv.at[hid],
            gi_ssem.at[d, part], gi_rsem.at[hid], (mp, dest),
        )

    def input_grad(*ds):
        total = jnp.zeros((BLOCK * len(ds), 512), F32)
        for p in range(2):
            c0, width = PHASES[p]
            for half in range(2):
                for mat in range(2):
                    left = [
                        gathered[p][half, 1 + mat, pl.ds(pl.multiple_of(d * BLOCK, BLOCK), BLOCK)] for d in ds
                    ]
                    left = jnp.concatenate(left) if len(ds) > 1 else left[0]
                    total += dot_nt(left, w_gu[half, mat, :, c0 : c0 + width])
        for i, d in enumerate(ds):
            gi_send[d] = encode(total[BLOCK * i : BLOCK * i + BLOCK])
            for part in range(2):
                @pl.when(hid != 2 * d + part)
                def _():
                    gi_copy(d, part).start()

    for p, m in pieces[:4]:
        reduce_first(p, m)
    pass_on(1)
    finish(1)
    for p, m in pieces[4:]:
        reduce_first(p, m)
    lax.fori_loop(1, 4, reduce_step, 0)
    for p, m in pieces:
        own[p][m] = partial(p, m, z)
    for p in range(2):
        activate(p)
        spread_first(p)
    for step in (1, 2, 3):
        for p in range(2):
            spread_next(p, step)
        if step == 1:
            pair_copy(0, 0).wait_recv()
            pair_copy(1, 0).wait_recv()
            input_grad(z)
        else:
            for p in range(2):
                pair_copy(p, step - 1).wait_recv()
                pair_copy(p, step + 2).wait_recv()
            input_grad(lax.rem(z + 9 - step, 8), lax.rem(z + step - 1, 8))
    for p in range(2):
        pair_copy(p, 3).wait_recv()
        pair_copy(p, 6).wait_recv()
    input_grad(lax.rem(z + 5, 8), lax.rem(z + 3, 8))
    for p in range(2):
        spread_last(p)
    for p in range(2):
        pair_copy(p, 7).wait_recv()
    input_grad(lax.rem(z + 4, 8))
    for p in range(2):
        for mat in range(2):
            saliency_gu(p, mat)
        saliency_d(p)

    total = decode(gi_send[hid // 2, pl.ds(pl.multiple_of(lax.rem(hid, 2) * 32, 32), 32)])
    for j in range(1, 16):
        slot = lax.rem(hid + j, 16)
        remote(
            gi_send.at[0, 0:32], gi_recv.at[slot], gi_ssem.at[0, 0], gi_rsem.at[slot], in_plane(j)
        ).wait_recv()
        total += decode(gi_recv[slot])
    gi_ref[...] = total.astype(BF16)

    for copy in copies:
        copy.wait_send()
    for p in range(2):
        for way in range(2):
            for m in range(3):
                first_copy(p, way, m).wait_send()
                for step in (1, 2, 3):
                    next_copy(p, way, step, m).wait_send()
                for step in range(4):
                    spread_copy(p, way, step, m).wait_send()
        for k in range(8):
            pair_copy(p, k).wait_send()

    def sent(d, _):
        for part in range(2):
            @pl.when(hid != 2 * d + part)
            def _():
                gi_copy(d, part).wait_send()
        return 0

    lax.fori_loop(0, 8, sent, 0)


def write_out(gi_in, gu_in, d_in, gi_ref, sg_ref, su_ref, sd_ref, sem):
    core = lax.rem(lax.axis_index("mp"), 2)
    copies = [pltpu.make_async_copy(gi_in, gi_ref, sem.at[6])]
    for half in range(2):
        at = pl.ds(pl.multiple_of((core + half * (1 - 2 * core)) * HALF, 128), HALF)
        for m, (src, dst) in enumerate((
            (gu_in.at[half, 0], sg_ref.at[:, at]),
            (gu_in.at[half, 1], su_ref.at[:, at]),
            (d_in.at[half], sd_ref.at[at, :]),
        )):
            copies.append(pltpu.make_async_copy(src, dst, sem.at[2 * m + half]))
    for copy in copies:
        copy.start()
    for copy in copies:
        copy.wait()


def local(tokens, grad_output, gate_weight, up_weight, down_weight):
    anywhere = pl.BlockSpec(memory_space=pl.ANY)
    dma = pltpu.SemaphoreType.DMA
    sizes = [width for _, width in PHASES]
    vmem = pl.BlockSpec(memory_space=pltpu.VMEM)
    results = pl.pallas_call(
        kernel,
        out_shape=(
            pltpu.VMEM((32, 512), BF16),
            pltpu.VMEM((2, 2, 512, HALF), BF16),
            pltpu.VMEM((2, HALF, 512), BF16),
        ),
        in_specs=[anywhere] * 5,
        out_specs=(vmem, vmem, vmem),
        scratch_shapes=[
            pltpu.VMEM((2, 4, 4, 32, 512), BF16),
            pltpu.VMEM((2, 4, 4, 32, 512), BF16),
            pltpu.VMEM((2, 2, 512, HALF), BF16),
            pltpu.VMEM((2, HALF, 512), BF16),
            pltpu.VMEM((2, 512, HALF), BF16),
            pltpu.VMEM((HALF, 512), BF16),
            *[pltpu.VMEM((2, 3, 3, BLOCK, width), BF16) for width in sizes],
            *[pltpu.VMEM((2, 4, 3, BLOCK, width), BF16) for width in sizes],
            *[pltpu.VMEM((3, BLOCK, width), BF16) for width in sizes],
            *[pltpu.VMEM((3, BLOCK, width), F32) for width in sizes],
            *[pltpu.VMEM((2, 3, 512, width), BF16) for width in sizes],
            pltpu.VMEM((8, BLOCK, 512), BF16),
            pltpu.VMEM((16, 32, 512), BF16),
            dma((8,)),
            dma((3,)),
            dma((3,)),
            dma((2, 2, 9)),
            dma((2, 2, 9)),
            dma((2, 2, 4)),
            dma((2, 2, 4)),
            dma((2, 2, 4, 3)),
            dma((2, 2, 4, 3)),
            dma((2, 2, 4, 3)),
            dma((2, 2, 4, 3)),
            dma((2, 8)),
            dma((2, 8)),
            dma((8, 2)),
            dma((16,)),
        ],
        compiler_params=pltpu.CompilerParams(
            collective_id=0, has_side_effects=True, vmem_limit_bytes=55 * 2**20
        ),
        cost_estimate=pl.CostEstimate(flops=7_516_192_768, bytes_accessed=11_010_048, transcendentals=2_000_000),
    )(tokens, grad_output, gate_weight, up_weight, down_weight)
    return pl.pallas_call(
        write_out,
        out_shape=(
            jax.ShapeDtypeStruct((32, 512), BF16),
            jax.ShapeDtypeStruct((512, 1792), BF16),
            jax.ShapeDtypeStruct((512, 1792), BF16),
            jax.ShapeDtypeStruct((1792, 512), BF16),
        ),
        in_specs=[anywhere] * 3,
        out_specs=(anywhere,) * 4,
        scratch_shapes=[dma((7,))],
        compiler_params=pltpu.CompilerParams(vmem_limit_bytes=2**20),
    )(*results)


def solution(mesh):
    return jax.shard_map(
        local,
        mesh=mesh,
        in_specs=(
            P("hidden", "mp"),
            P("hidden", "mp"),
            P("mp", "hidden"),
            P("mp", "hidden"),
            P("hidden", "mp"),
        ),
        out_specs=(P("hidden", "mp"), P("mp", "hidden"), P("mp", "hidden"), P("hidden", "mp")),
        check_vma=False,
    )
```

time: 117 us -> 97.6 us (0.83); the launches traced: 115 us -> 97.5 us
  Pallas kernels: 107 us -> 96.9 us
  local copies, waits for them, and re-layouts: 7.75 us -> 0 us
    pallas_call x1 -> x2, Pallas kernels: 107 us -> 96.9 us  [the longest x1 94.3 us: local(): pl.pallas_call(kernel, out_shape=(pltpu.VMEM((32, 512), BF16), pltpu.VMEM...]
    unnamed x8 -> x0, local copies, waits for them, and re-layouts: 7.75 us -> none
where the time goes in v2:
time: 97.6 us; the launch traced here: 97.5 us
  Pallas kernels  96.9 us (99%)
    pallas_call x1, Pallas kernels, local(): pl.pallas_call(kernel, out_shape=(pltpu.VMEM((32, 512), BF16), pltpu.VMEM...  94.3 us
    pallas_call x1, Pallas kernels, local(): pl.pallas_call(write_out, out_shape=(jax.ShapeDtypeStruct((32, 512), BF16...  2.51 us

profile of v2, /device:TPU:1, one launch (start us, length us, event | category | flops | bytes accessed | tf_op | source)
XLA Modules:
  0.0 97.5 jit_solution(6972022293053267857)
XLA Ops:
  0.6 94.3 %shard_map.84 = (bf16[32,512]{1,0:T(8,128)(2,1)S(1)}, bf16[2,2,512,896]{3,2,1,0:T(8,128)(2,1)S(1)}, bf16[2,896,512]{2,1,0:T(8,128)(2,1)S(1)}) custom-call(bf16[32,512]{1,0:T(8,128)(2,1)} %tok_ref.1, bf16[32,512]{1,0:T(8,128)(2,1)} %go_ref.1, bf16[512,1792]{1,0:T(8,128)(2,1)} %wg_ref.1, bf16[512,1792]{1,0:T(8,128)(2,1)} %wu_ref.1, bf16[1792,512]{1,0:T(8,128)(2,1)} %wd_ref.1), custom_call_target="tpu_custom_call" | custom-call | flops 7516192768 | bytes 11010048 | tf_op jit(solution)/shard_map/pallas_call | solution.py:436
  95.0 2.5 %shard_map.85 = (bf16[32,512]{1,0:T(8,128)(2,1)}, bf16[512,1792]{1,0:T(8,128)(2,1)}, bf16[512,1792]{1,0:T(8,128)(2,1)}, bf16[1792,512]{1,0:T(8,128)(2,1)}) custom-call(bf16[32,512]{1,0:T(8,128)(2,1)S(1)} %get-tuple-element.7.gi_in, bf16[2,2,512,896]{3,2,1,0:T(8,128)(2,1)S(1)} %get-tuple-element.8.gu_in, bf16[2,896,512]{2,1,0:T(8,128)(2,1)S(1)} %get-tuple-element.9.d_in), custom_call_target="tpu_custom_call" | custom-call | tf_op jit(solution)/shard_map/pallas_call | solution.py:480

commit v3 on v0

v3 whole, which is shorter than its diff:
```python
import jax
import jax.numpy as jnp
from jax import lax
from jax.experimental import pallas as pl
from jax.experimental.pallas import tpu as pltpu
from jax.sharding import PartitionSpec as P

MESH = pl.DeviceIdType.MESH
F32 = jnp.float32
BF16 = jnp.bfloat16
HALF = 896
SHARE = 16
ROW = 128
STEPS = (0, 1, 3, 2)
START = (0.0, 2.2, 2.3, 2.4)
SPREAD = (6.0, 6.55, 6.6, 6.75)


def encode(value):
    return (value * jnp.abs(value)).astype(BF16)


def decode(sent):
    square = sent.astype(F32)
    size = jnp.abs(square)
    root = size * lax.rsqrt(jnp.maximum(size, 1e-36))
    return jnp.where(square < 0, -root, root)


def dot_nt(left, right):
    return lax.dot_general(left, right, (((1,), (1,)), ((), ())), preferred_element_type=F32)


def dot_tn(left, right):
    return lax.dot_general(left, right, (((0,), (0,)), ((), ())), preferred_element_type=F32)


def kernel(
    tok_ref, go_ref, wg_ref, wu_ref, wd_ref,
    gi_ref, out_gu, out_d,
    act_in, act_px, w_gu, w_d, px_gu, px_d,
    part, rs_send, rs_recv, gathered, gi_send, gi_recv,
    load_sem, px_send, px_recv, tok_send, tok_recv, share_send, share_recv,
    rs_ssem, rs_rsem, ag_ssem, ag_rsem, pair_send, pair_recv, gi_ssem, gi_rsem,
):
    mp, hid = lax.axis_index("mp"), lax.axis_index("hidden")
    z, core = mp // 2, mp % 2
    y, x = hid // 4, hid % 4

    def remote(src, dst, ssem, rsem, device):
        return pltpu.make_async_remote_copy(
            src_ref=src, dst_ref=dst, send_sem=ssem, recv_sem=rsem, device_id=device, device_id_type=MESH
        )

    def ring(way):
        return (lax.rem(z + 1 + 6 * way, 8) * 2 + core, hid)

    partner = (z * 2 + (1 - core), hid)

    def in_plane(j):
        return (mp, lax.rem(hid + j, 16))

    def along_x(step):
        return (mp, y * 4 + lax.rem(x + step, 4))

    def along_y(step):
        return (mp, lax.rem(y + step, 4) * 4 + x)

    own_col = pl.multiple_of(core * HALF, 128)
    other_col = pl.multiple_of((1 - core) * HALF, 128)

    loads = []

    def load(src, dst):
        copy = pltpu.make_async_copy(src, dst, load_sem.at[len(loads)])
        copy.start()
        loads.append(copy)

    load(tok_ref, act_in.at[0, 0, x])
    load(go_ref, act_in.at[1, 0, x])
    for half, col in ((0, own_col), (1, other_col)):
        load(wg_ref.at[:, pl.ds(col, HALF)], w_gu.at[half, 0])
        load(wu_ref.at[:, pl.ds(col, HALF)], w_gu.at[half, 1])
        load(wd_ref.at[pl.ds(col, HALF), :], w_d.at[half])

    barrier = pltpu.get_barrier_semaphore()
    for j in range(1, 16):
        pl.semaphore_signal(barrier, inc=1, device_id=in_plane(j), device_id_type=MESH)
    for device in (ring(0), ring(1), partner):
        pl.semaphore_signal(barrier, inc=1, device_id=device, device_id_type=MESH)
    pl.semaphore_wait(barrier, 18)

    copies = []

    def begin(copy):
        copy.start()
        copies.append(copy)
        return copy

    low, high = slice(0, 256), slice(256, 512)
    row, column, wide, far, shares = {}, {}, {}, {}, {}
    for a, source in enumerate((tok_ref, go_ref)):
        for j, step in enumerate((2, 1, 3)):
            row[a, j] = begin(remote(
                source, act_in.at[a, 0, x], tok_send.at[a, j], tok_recv.at[a, j], along_x(step)
            ))
        for j, (step, q) in enumerate(((2, 3), (1, 2), (3, 1))):
            column[a, j] = begin(remote(
                source.at[:, high], act_in.at[a, q, x, :, high],
                tok_send.at[a, 3 + j], tok_recv.at[a, 3 + j], along_y(step),
            ))
    px_copies = []
    for i, (src, dst) in enumerate((
        (wg_ref.at[:, pl.ds(other_col, HALF)], px_gu.at[0]),
        (wu_ref.at[:, pl.ds(other_col, HALF)], px_gu.at[1]),
        (wd_ref.at[pl.ds(other_col, HALF), :], px_d),
    )):
        px_copies.append(begin(remote(src, dst, px_send.at[i], px_recv.at[i], partner)))

    def share(a, i):
        q = slice(0, 1) if i == 0 else slice(1, 4)
        shares[a, i] = begin(remote(
            act_in.at[a, q], act_px.at[a, q], share_send.at[a, i], share_recv.at[a, i], partner
        ))

    def send_row(a):
        loads[a].wait()
        for j in range(3):
            row[a, j].wait_recv()
        share(a, 0)
        for way in (a, 1 - a):
            wide[a, 0, way] = begin(remote(
                act_in.at[a, 0, :, :, low], act_in.at[a, 2 - way, :, :, low],
                tok_send.at[a, 6 + way], tok_recv.at[a, 6 + way], along_y(1 + 2 * way),
            ))

    def send_column(a):
        for j in range(3):
            column[a, j].wait_recv()
        for way in (a, 1 - a):
            ref = act_in.at[a, 1:4, x, :, high]
            wide[a, 1, way] = begin(remote(
                ref, ref, tok_send.at[a, 8 + way], tok_recv.at[a, 8 + way], along_x(1 + 2 * way)
            ))

    def pass_on(a):
        wide[a, 0, a].wait_recv()
        far[a, 0] = begin(remote(
            act_in.at[a, 2 - a, :, :, low], act_in.at[a, 3, :, :, low],
            tok_send.at[a, 10], tok_recv.at[a, 10], along_y(1 + 2 * a),
        ))
        wide[a, 1, a].wait_recv()
        ref = act_in.at[a, 1:4, lax.rem(x + 3 - 2 * a, 4), :, high]
        far[a, 1] = begin(remote(ref, ref, tok_send.at[a, 11], tok_recv.at[a, 11], along_x(1 + 2 * a)))

    def share_far(a):
        for axis in range(2):
            wide[a, axis, 1 - a].wait_recv()
            far[a, axis].wait_recv()
        share(a, 1)

    def multiply(q):
        for m in range(3):
            a = m // 2
            if m != 1 and q < 2:
                shares[a, q].wait_recv()
            ours, theirs = act_in[a, q].reshape(ROW, 512), act_px[a, q].reshape(ROW, 512)
            if q == 0:
                px_copies[m].wait_recv()
            if m == 2:
                part[q, m] = dot_nt(ours, w_d[0]) + dot_nt(theirs, px_d[...])
            else:
                part[q, m] = jnp.dot(ours, w_gu[0, m], preferred_element_type=F32) + jnp.dot(
                    theirs, px_gu[m], preferred_element_type=F32
                )

    def sum_copy(q, way, step):
        return remote(
            rs_send.at[q, way, step], rs_recv.at[q, way, step],
            rs_ssem.at[q, way, step], rs_rsem.at[q, way, step], ring(way),
        )

    def sum_ways(q, step):
        return (q % 2,) if step == 0 else (q % 2, 1 - q % 2)

    def reduce(q, step):
        for way in sum_ways(q, step):
            distance = 4 - step
            d = lax.rem(z + (distance if way == 0 else 8 - distance), 8)
            total = part[q, :, pl.ds(pl.multiple_of(d * SHARE, SHARE), SHARE)]
            if step > 0 and way in sum_ways(q, step - 1):
                sum_copy(q, way, step - 1).wait_recv()
                total += decode(rs_recv[q, way, step - 1])
            rs_send[q, way, step] = encode(total)
            sum_copy(q, way, step).start()

    def rows(q, d):
        return pl.ds(pl.multiple_of(q * ROW + d * SHARE, SHARE), SHARE)

    def activate(q):
        sums = part[q, :, pl.ds(pl.multiple_of(z * SHARE, SHARE), SHARE)]
        for way in sum_ways(q, 3):
            sum_copy(q, way, 3).wait_recv()
            sums += decode(rs_recv[q, way, 3])
        gate, up, grad_hidden = sums[0], sums[1], sums[2]
        sig = jax.nn.sigmoid(gate)
        silu_gate = gate * sig
        gathered[0, 0, rows(q, z)] = (silu_gate * up).astype(BF16)
        gathered[0, 1, rows(q, z)] = (grad_hidden * up * sig * (1.0 + gate * (1.0 - sig))).astype(BF16)
        gathered[0, 2, rows(q, z)] = (grad_hidden * silu_gate).astype(BF16)

    def spread_copy(q, way, step):
        ref = gathered.at[0, :, rows(q, lax.rem(z + (8 - step if way == 0 else step), 8))]
        return remote(ref, ref, ag_ssem.at[q, way, step], ag_rsem.at[q, way, step], ring(way))

    def spread_ways(q, step):
        return (q % 2,) if step == 3 else (q % 2, 1 - q % 2)

    def pair_copy(q, k):
        at = rows(q, lax.rem(z + (0, 7, 6, 5, 1, 2, 3, 4)[k], 8))
        return remote(
            gathered.at[0, :, at], gathered.at[1, :, at], pair_send.at[q, k], pair_recv.at[q, k], partner
        )

    def spread(q, step):
        if step == 0:
            activate(q)
        for way in (q % 2, 1 - q % 2):
            if 0 < step < 4 or (step == 4 and way == q % 2):
                spread_copy(q, way, step - 1).wait_recv()
            if step < 4 and way in spread_ways(q, step):
                spread_copy(q, way, step).start()
        if step == 0:
            pair_copy(q, 0).start()
        elif step < 4:
            pair_copy(q, step).start()
            pair_copy(q, 3 + step).start()
        else:
            pair_copy(q, 7).start()

    def gi_copy(q, d):
        return remote(
            gi_send.at[d, q], gi_recv.at[hid, lax.rem(d, 2)], gi_ssem.at[d, q],
            gi_rsem.at[hid, lax.rem(d, 2)], (mp, lax.rem(y + STEPS[q], 4) * 4 + d // 2),
        )

    def gi_each(q, d, act):
        if q == 0:
            pl.when(x != d // 2)(lambda: act(gi_copy(q, d)))
        else:
            act(gi_copy(q, d))

    def input_grad(distance):
        places = ((0, z),) if distance == 0 else ((7, lax.rem(z + 4, 8)),) if distance == 4 else (
            (distance, lax.rem(z + 8 - distance, 8)), (3 + distance, lax.rem(z + distance, 8))
        )
        for k, _ in places:
            for q in range(4):
                pair_copy(q, k).wait_recv()
        total = jnp.zeros((4 * SHARE * len(places), 512), F32)
        for half in range(2):
            for mat in range(2):
                left = jnp.concatenate([gathered[half, 1 + mat, rows(q, d)] for _, d in places for q in range(4)])
                total += dot_nt(left, w_gu[half, mat])
        for i, (_, d) in enumerate(places):
            for q in range(4):
                start = (4 * i + q) * SHARE
                gi_send[d, q] = encode(total[start : start + SHARE])
                gi_each(q, d, lambda copy: copy.start())

    def saliency(half, _):
        tokens = act_in[0].reshape(512, 512)
        for mat in range(2):
            for cols in (slice(0, 512), slice(512, HALF)):
                grads = dot_tn(tokens, gathered[half, 1 + mat, :, cols])
                out_gu[half, mat, :, cols] = jnp.abs(w_gu[half, mat, :, cols].astype(F32) * grads).astype(BF16)
        for cols in (slice(0, 512), slice(512, HALF)):
            grads = dot_tn(gathered[half, 0, :, cols], act_in[1].reshape(512, 512))
            out_d[half, cols, :] = jnp.abs(w_d[half, cols, :].astype(F32) * grads).astype(BF16)
        return 0

    send_row(0)
    send_row(1)
    for copy in loads[2:]:
        copy.wait()
    events = [
        (-0.05, 0, lambda: (send_column(0), send_column(1))),
        (0.9, 0, lambda: (pass_on(0), pass_on(1))),
        (1.9, 0, lambda: (share_far(0), share_far(1))),
    ]
    for q in range(4):
        events.append((START[q] - 0.1, q, lambda q=q: multiply(q)))
        for step in range(4):
            events.append((START[q] + step, q, lambda q=q, step=step: reduce(q, step)))
        for step in range(5):
            events.append((SPREAD[q] + step, q, lambda q=q, step=step: spread(q, step)))
    for distance, when in enumerate((1.05, 2.05, 3.05, 3.5, 4.5)):
        events.append((SPREAD[3] + when, 4, lambda distance=distance: input_grad(distance)))
    for _, _, event in sorted(events, key=lambda e: e[:2]):
        event()
    lax.fori_loop(0, 2, saliency, 0)

    totals = [decode(gi_send[2 * x + i, 0]) for i in range(2)]
    for j in range(1, 16):
        slot = lax.rem(hid + j, 16)
        for i in range(2):
            remote(
                gi_send.at[0, 0], gi_recv.at[slot, i], gi_ssem.at[0, 0], gi_rsem.at[slot, i], in_plane(j)
            ).wait_recv()
            totals[i] += decode(gi_recv[slot, i])
    for i in range(2):
        gi_ref[SHARE * i : SHARE * i + SHARE] = totals[i].astype(BF16)

    for copy in copies:
        copy.wait_send()
    for q in range(4):
        for step in range(4):
            for way in sum_ways(q, step):
                sum_copy(q, way, step).wait_send()
            for way in spread_ways(q, step):
                spread_copy(q, way, step).wait_send()
        for k in range(8):
            pair_copy(q, k).wait_send()
        for d in range(8):
            gi_each(q, d, lambda copy: copy.wait_send())


def write_out(gi_in, gu_in, d_in, gi_ref, sg_ref, su_ref, sd_ref, sem):
    core = lax.rem(lax.axis_index("mp"), 2)
    copies = [pltpu.make_async_copy(gi_in, gi_ref, sem.at[6])]
    for half in range(2):
        at = pl.ds(pl.multiple_of((core + half * (1 - 2 * core)) * HALF, 128), HALF)
        for m, (src, dst) in enumerate((
            (gu_in.at[half, 0], sg_ref.at[:, at]),
            (gu_in.at[half, 1], su_ref.at[:, at]),
            (d_in.at[half], sd_ref.at[at, :]),
        )):
            copies.append(pltpu.make_async_copy(src, dst, sem.at[2 * m + half]))
    for copy in copies:
        copy.start()
    for copy in copies:
        copy.wait()


def local(tokens, grad_output, gate_weight, up_weight, down_weight):
    anywhere = pl.BlockSpec(memory_space=pl.ANY)
    dma = pltpu.SemaphoreType.DMA
    vmem = pl.BlockSpec(memory_space=pltpu.VMEM)
    results = pl.pallas_call(
        kernel,
        out_shape=(
            pltpu.VMEM((32, 512), BF16),
            pltpu.VMEM((2, 2, 512, HALF), BF16),
            pltpu.VMEM((2, HALF, 512), BF16),
        ),
        in_specs=[anywhere] * 5,
        out_specs=(vmem, vmem, vmem),
        scratch_shapes=[
            pltpu.VMEM((2, 4, 4, 32, 512), BF16),
            pltpu.VMEM((2, 4, 4, 32, 512), BF16),
            pltpu.VMEM((2, 2, 512, HALF), BF16),
            pltpu.VMEM((2, HALF, 512), BF16),
            pltpu.VMEM((2, 512, HALF), BF16),
            pltpu.VMEM((HALF, 512), BF16),
            pltpu.VMEM((4, 3, ROW, HALF), F32),
            pltpu.VMEM((4, 2, 4, 3, SHARE, HALF), BF16),
            pltpu.VMEM((4, 2, 4, 3, SHARE, HALF), BF16),
            pltpu.VMEM((2, 3, 512, HALF), BF16),
            pltpu.VMEM((8, 4, SHARE, 512), BF16),
            pltpu.VMEM((16, 2, SHARE, 512), BF16),
            dma((8,)),
            dma((3,)),
            dma((3,)),
            dma((2, 12)),
            dma((2, 12)),
            dma((2, 2)),
            dma((2, 2)),
            dma((4, 2, 4)),
            dma((4, 2, 4)),
            dma((4, 2, 4)),
            dma((4, 2, 4)),
            dma((4, 8)),
            dma((4, 8)),
            dma((8, 4)),
            dma((16, 2)),
        ],
        compiler_params=pltpu.CompilerParams(
            collective_id=0, has_side_effects=True, vmem_limit_bytes=55 * 2**20
        ),
        cost_estimate=pl.CostEstimate(flops=7_516_192_768, bytes_accessed=11_010_048, transcendentals=2_000_000),
    )(tokens, grad_output, gate_weight, up_weight, down_weight)
    return pl.pallas_call(
        write_out,
        out_shape=(
            jax.ShapeDtypeStruct((32, 512), BF16),
            jax.ShapeDtypeStruct((512, 1792), BF16),
            jax.ShapeDtypeStruct((512, 1792), BF16),
            jax.ShapeDtypeStruct((1792, 512), BF16),
        ),
        in_specs=[anywhere] * 3,
        out_specs=(anywhere,) * 4,
        scratch_shapes=[dma((7,))],
        compiler_params=pltpu.CompilerParams(vmem_limit_bytes=2**20),
    )(*results)


def solution(mesh):
    return jax.shard_map(
        local,
        mesh=mesh,
        in_specs=(
            P("hidden", "mp"),
            P("hidden", "mp"),
            P("mp", "hidden"),
            P("mp", "hidden"),
            P("hidden", "mp"),
        ),
        out_specs=(P("hidden", "mp"), P("mp", "hidden"), P("mp", "hidden"), P("hidden", "mp")),
        check_vma=False,
    )
```

time: 309 us -> 92.6 us (0.30)
  waiting for transfers between devices: 206 us -> 0 us
  Pallas kernels: 0 us -> 91.7 us
  blocking collectives: 37.4 us -> 0 us
  matrix products: 27.7 us -> 0 us
  local copies, waits for them, and re-layouts: 15.9 us -> 0 us
  between operations: 14.1 us -> 0.8 us
  other arithmetic: 6.56 us -> 0 us
    psum x1 -> x0, waiting for transfers between devices: 158 us -> none  [local(): gate, up, grad_hidden = lax.psum((gate_part, up_part, hid_part), 'mp')]
    pallas_call x0 -> x2, Pallas kernels: none -> 91.7 us  [the longest x1 89.2 us: local(): pl.pallas_call(kernel, out_shape=(pltpu.VMEM((32, 512), BF16), pltpu.VMEM...]
    reduce_scatter x1 -> x0, waiting for transfers between devices: 48.3 us -> none  [local(): lax.psum_scatter(first + second, 'hidden', scatter_dimension=0, tiled=True)]
    all_gather x2 -> x0, blocking collectives: 37.4 us -> none  [the longest x1 20 us: local(): lax.all_gather(tokens, 'hidden', axis=0, tiled=True)]
    dot_general x8 -> x0, matrix products: 27.7 us -> none  [the longest x3 13.9 us: saliency(): lax.dot_general(left, right, (((0,), (0,)), ((), ())), preferred_element_...]
    unnamed x22 -> x0, local copies, waits for them, and re-layouts: 15.9 us -> none
    convert_element_type x2 -> x0, other arithmetic: 6.56 us -> none  [the longest x1 5.1 us: activate(): grad_up = (grad_hidden * silu_gate).astype(jnp.bfloat16)]
  transfers between devices with their start and end apart: 2 -> 0, of which waited for: 2 -> 0; matrix products, arithmetic and copies ran while one was open for 9% -> 0% of each run, Pallas kernels for 0% -> 0%
where the time goes in v3:
time: 92.6 us; the launch traced here: 92.5 us
  Pallas kernels  91.7 us (99%)
    pallas_call x1, Pallas kernels, local(): pl.pallas_call(kernel, out_shape=(pltpu.VMEM((32, 512), BF16), pltpu.VMEM...  89.2 us
    pallas_call x1, Pallas kernels, local(): pl.pallas_call(write_out, out_shape=(jax.ShapeDtypeStruct((32, 512), BF16...  2.51 us

profile of v3, /device:TPU:1, one launch (start us, length us, event | category | flops | bytes accessed | tf_op | source)
XLA Modules:
  0.0 92.5 jit_solution(9188977996140019620)
XLA Ops:
  0.6 89.2 %shard_map.84 = (bf16[32,512]{1,0:T(8,128)(2,1)S(1)}, bf16[2,2,512,896]{3,2,1,0:T(8,128)(2,1)S(1)}, bf16[2,896,512]{2,1,0:T(8,128)(2,1)S(1)}) custom-call(bf16[32,512]{1,0:T(8,128)(2,1)} %tok_ref.1, bf16[32,512]{1,0:T(8,128)(2,1)} %go_ref.1, bf16[512,1792]{1,0:T(8,128)(2,1)} %wg_ref.1, bf16[512,1792]{1,0:T(8,128)(2,1)} %wu_ref.1, bf16[1792,512]{1,0:T(8,128)(2,1)} %wd_ref.1), custom_call_target="tpu_custom_call" | custom-call | flops 7516192768 | bytes 11010048 | tf_op jit(solution)/shard_map/pallas_call | solution.py:349
  89.8 2.5 %shard_map.85 = (bf16[32,512]{1,0:T(8,128)(2,1)}, bf16[512,1792]{1,0:T(8,128)(2,1)}, bf16[512,1792]{1,0:T(8,128)(2,1)}, bf16[1792,512]{1,0:T(8,128)(2,1)}) custom-call(bf16[32,512]{1,0:T(8,128)(2,1)S(1)} %get-tuple-element.7.gi_in, bf16[2,2,512,896]{3,2,1,0:T(8,128)(2,1)S(1)} %get-tuple-element.8.gu_in, bf16[2,896,512]{2,1,0:T(8,128)(2,1)S(1)} %get-tuple-element.9.d_in), custom_call_target="tpu_custom_call" | custom-call | tf_op jit(solution)/shard_map/pallas_call | solution.py:392

commit v4 on v3

--- a/solution.py
+++ b/solution.py
@@ -78,10 +78,12 @@
 
     load(tok_ref, act_in.at[0, 0, x])
     load(go_ref, act_in.at[1, 0, x])
-    for half, col in ((0, own_col), (1, other_col)):
+    def load_half(half, col):
         load(wg_ref.at[:, pl.ds(col, HALF)], w_gu.at[half, 0])
         load(wu_ref.at[:, pl.ds(col, HALF)], w_gu.at[half, 1])
         load(wd_ref.at[pl.ds(col, HALF), :], w_d.at[half])
+
+    load_half(0, own_col)
 
     barrier = pltpu.get_barrier_semaphore()
     for j in range(1, 16):
@@ -104,6 +106,7 @@
             row[a, j] = begin(remote(
                 source, act_in.at[a, 0, x], tok_send.at[a, j], tok_recv.at[a, j], along_x(step)
             ))
+    for a, source in enumerate((tok_ref, go_ref)):
         for j, (step, q) in enumerate(((2, 3), (1, 2), (3, 1))):
             column[a, j] = begin(remote(
                 source.at[:, high], act_in.at[a, q, x, :, high],
@@ -268,22 +271,24 @@
                 gi_send[d, q] = encode(total[start : start + SHARE])
                 gi_each(q, d, lambda copy: copy.start())
 
-    def saliency(half, _):
+    def saliency_in(half, mat):
         tokens = act_in[0].reshape(512, 512)
-        for mat in range(2):
-            for cols in (slice(0, 512), slice(512, HALF)):
-                grads = dot_tn(tokens, gathered[half, 1 + mat, :, cols])
-                out_gu[half, mat, :, cols] = jnp.abs(w_gu[half, mat, :, cols].astype(F32) * grads).astype(BF16)
+        for cols in (slice(0, 512), slice(512, HALF)):
+            grads = dot_tn(tokens, gathered[half, 1 + mat, :, cols])
+            out_gu[half, mat, :, cols] = jnp.abs(w_gu[half, mat, :, cols].astype(F32) * grads).astype(BF16)
+
+    def saliency_down(half):
         for cols in (slice(0, 512), slice(512, HALF)):
             grads = dot_tn(gathered[half, 0, :, cols], act_in[1].reshape(512, 512))
             out_d[half, cols, :] = jnp.abs(w_d[half, cols, :].astype(F32) * grads).astype(BF16)
-        return 0
 
     send_row(0)
     send_row(1)
     for copy in loads[2:]:
         copy.wait()
+    load_half(1, other_col)
     events = [
+        (4.0, 0, lambda: [copy.wait() for copy in loads[5:]]),
         (-0.05, 0, lambda: (send_column(0), send_column(1))),
         (0.9, 0, lambda: (pass_on(0), pass_on(1))),
         (1.9, 0, lambda: (share_far(0), share_far(1))),
@@ -296,9 +301,13 @@
             events.append((SPREAD[q] + step, q, lambda q=q, step=step: spread(q, step)))
     for distance, when in enumerate((1.05, 2.05, 3.05, 3.5, 4.5)):
         events.append((SPREAD[3] + when, 4, lambda distance=distance: input_grad(distance)))
+    events.append((SPREAD[3] + 4.2, 4, lambda: (saliency_in(0, 0), saliency_in(0, 1))))
     for _, _, event in sorted(events, key=lambda e: e[:2]):
         event()
-    lax.fori_loop(0, 2, saliency, 0)
+    saliency_down(0)
+    for mat in range(2):
+        saliency_in(1, mat)
+    saliency_down(1)
 
     totals = [decode(gi_send[2 * x + i, 0]) for i in range(2)]
     for j in range(1, 16):

time: 92.6 us -> 92.1 us (level)
  Pallas kernels: 91.7 us -> 90.4 us
    pallas_call x1, Pallas kernels: 89.2 us -> 87.9 us  [local(): pl.pallas_call(kernel, out_shape=(pltpu.VMEM((32, 512), BF16), pltpu.VMEM...]
where the time goes in v4:
time: 92.1 us; the launch traced here: 91.2 us
  Pallas kernels  90.4 us (98%)
    pallas_call x1, Pallas kernels, local(): pl.pallas_call(kernel, out_shape=(pltpu.VMEM((32, 512), BF16), pltpu.VMEM...  87.9 us
    pallas_call x1, Pallas kernels, local(): pl.pallas_call(write_out, out_shape=(jax.ShapeDtypeStruct((32, 512), BF16...  2.51 us

profile of v4, /device:TPU:1, one launch (start us, length us, event | category | flops | bytes accessed | tf_op | source)
XLA Modules:
  0.0 91.2 jit_solution(495942599764584259)
XLA Ops:
  0.6 87.9 %shard_map.84 = (bf16[32,512]{1,0:T(8,128)(2,1)S(1)}, bf16[2,2,512,896]{3,2,1,0:T(8,128)(2,1)S(1)}, bf16[2,896,512]{2,1,0:T(8,128)(2,1)S(1)}) custom-call(bf16[32,512]{1,0:T(8,128)(2,1)} %tok_ref.1, bf16[32,512]{1,0:T(8,128)(2,1)} %go_ref.1, bf16[512,1792]{1,0:T(8,128)(2,1)} %wg_ref.1, bf16[512,1792]{1,0:T(8,128)(2,1)} %wu_ref.1, bf16[1792,512]{1,0:T(8,128)(2,1)} %wd_ref.1), custom_call_target="tpu_custom_call" | custom-call | flops 7516192768 | bytes 11010048 | tf_op jit(solution)/shard_map/pallas_call | solution.py:358
  88.6 2.5 %shard_map.85 = (bf16[32,512]{1,0:T(8,128)(2,1)}, bf16[512,1792]{1,0:T(8,128)(2,1)}, bf16[512,1792]{1,0:T(8,128)(2,1)}, bf16[1792,512]{1,0:T(8,128)(2,1)}) custom-call(bf16[32,512]{1,0:T(8,128)(2,1)S(1)} %get-tuple-element.7.gi_in, bf16[2,2,512,896]{3,2,1,0:T(8,128)(2,1)S(1)} %get-tuple-element.8.gu_in, bf16[2,896,512]{2,1,0:T(8,128)(2,1)S(1)} %get-tuple-element.9.d_in), custom_call_target="tpu_custom_call" | custom-call | tf_op jit(solution)/shard_map/pallas_call | solution.py:401

commit v5 on v4

--- a/solution.py
+++ b/solution.py
@@ -113,12 +113,13 @@
                 tok_send.at[a, 3 + j], tok_recv.at[a, 3 + j], along_y(step),
             ))
     px_copies = []
-    for i, (src, dst) in enumerate((
-        (wg_ref.at[:, pl.ds(other_col, HALF)], px_gu.at[0]),
-        (wu_ref.at[:, pl.ds(other_col, HALF)], px_gu.at[1]),
-        (wd_ref.at[pl.ds(other_col, HALF), :], px_d),
-    )):
+
+    def exchange(src, dst):
+        i = len(px_copies)
         px_copies.append(begin(remote(src, dst, px_send.at[i], px_recv.at[i], partner)))
+
+    exchange(wg_ref.at[:, pl.ds(other_col, HALF)], px_gu.at[0])
+    exchange(wu_ref.at[:, pl.ds(other_col, HALF)], px_gu.at[1])
 
     def share(a, i):
         q = slice(0, 1) if i == 0 else slice(1, 4)
@@ -283,6 +284,7 @@
             out_d[half, cols, :] = jnp.abs(w_d[half, cols, :].astype(F32) * grads).astype(BF16)
 
     send_row(0)
+    exchange(wd_ref.at[pl.ds(other_col, HALF), :], px_d)
     send_row(1)
     for copy in loads[2:]:
         copy.wait()

time: 92.1 us -> 92.5 us (level)
  no operation moved by 1% of the time
where the time goes in v5:
time: 92.5 us; the launch traced here: 91.4 us
  Pallas kernels  90.6 us (98%)
    pallas_call x1, Pallas kernels, local(): pl.pallas_call(kernel, out_shape=(pltpu.VMEM((32, 512), BF16), pltpu.VMEM...  88.1 us
    pallas_call x1, Pallas kernels, local(): pl.pallas_call(write_out, out_shape=(jax.ShapeDtypeStruct((32, 512), BF16...  2.51 us

profile of v5, /device:TPU:1, one launch (start us, length us, event | category | flops | bytes accessed | tf_op | source)
XLA Modules:
  0.0 91.4 jit_solution(3182735922306885153)
XLA Ops:
  0.6 88.1 %shard_map.84 = (bf16[32,512]{1,0:T(8,128)(2,1)S(1)}, bf16[2,2,512,896]{3,2,1,0:T(8,128)(2,1)S(1)}, bf16[2,896,512]{2,1,0:T(8,128)(2,1)S(1)}) custom-call(bf16[32,512]{1,0:T(8,128)(2,1)} %tok_ref.1, bf16[32,512]{1,0:T(8,128)(2,1)} %go_ref.1, bf16[512,1792]{1,0:T(8,128)(2,1)} %wg_ref.1, bf16[512,1792]{1,0:T(8,128)(2,1)} %wu_ref.1, bf16[1792,512]{1,0:T(8,128)(2,1)} %wd_ref.1), custom_call_target="tpu_custom_call" | custom-call | flops 7516192768 | bytes 11010048 | tf_op jit(solution)/shard_map/pallas_call | solution.py:360
  88.8 2.5 %shard_map.85 = (bf16[32,512]{1,0:T(8,128)(2,1)}, bf16[512,1792]{1,0:T(8,128)(2,1)}, bf16[512,1792]{1,0:T(8,128)(2,1)}, bf16[1792,512]{1,0:T(8,128)(2,1)}) custom-call(bf16[32,512]{1,0:T(8,128)(2,1)S(1)} %get-tuple-element.7.gi_in, bf16[2,2,512,896]{3,2,1,0:T(8,128)(2,1)S(1)} %get-tuple-element.8.gu_in, bf16[2,896,512]{2,1,0:T(8,128)(2,1)S(1)} %get-tuple-element.9.d_in), custom_call_target="tpu_custom_call" | custom-call | tf_op jit(solution)/shard_map/pallas_call | solution.py:403
